TPU v7x, 512 devices: a whole 4x4x16 slice. The times are simulated.
512 devices in a mesh: feat: 64 (over z_hi, x, y, core), samp: 8 (over z_lo).
Axes of the slice: x: 4, y: 4, z: 16 (z_hi: 2, z_lo: 8; z = z_hi * 8 + z_lo), core: 2. Of those that a mesh axis runs over, the one named last changes fastest.
Arguments:
- samples: bfloat16 [4096, 8192], P('feat', 'samp'), may hold values from -6 to 6
- factors: bfloat16 [4096, 512], P('feat'), may hold values from -0.0546875 to 0.0546875
Outputs:
- factor_grad: float32 [4096, 512], P(('feat', 'samp'))
All inputs are finite; a program needn't handle non-finite values.
Results may differ from a plain program's by a relative error of at most 0.0017.
Values may be sent and summed in bfloat16 or wider, within the bound.
A program may use at most 64 MiB of HBM per device.

v0:
```python
import jax
import jax.numpy as jnp
from jax import lax
from jax.sharding import PartitionSpec as P


def contract_rows(left, right):
    return lax.dot_general(
        left, right, (((0,), (0,)), ((), ())), preferred_element_type=jnp.float32
    )


def on_device(samples, factors):
    samp_count = lax.axis_size("samp")
    partial_proj = contract_rows(samples, factors)
    proj = lax.psum(partial_proj, "feat")
    squared = (proj * proj).astype(jnp.bfloat16)
    data_term = jnp.dot(samples, squared, preferred_element_type=jnp.float32)
    gram = lax.psum(contract_rows(factors, factors), "feat")
    gram_sq = gram * gram
    own_rows = factors.shape[0] // samp_count
    first = lax.axis_index("samp") * own_rows
    own_factors = lax.dynamic_slice_in_dim(factors, first, own_rows, 0)
    model_term = jnp.dot(own_factors.astype(jnp.float32), gram_sq, precision=lax.Precision.HIGHEST)
    total = lax.psum(data_term, "samp")
    summed = lax.dynamic_slice_in_dim(total, first, own_rows, 0)
    sample_total = samples.shape[1] * samp_count
    return 6.0 * model_term - 6.0 / sample_total * summed


def solution(mesh):
    in_specs = (P("feat", "samp"), P("feat", None))
    out_specs = P(("feat", "samp"), None)
    return jax.shard_map(
        on_device, mesh=mesh, in_specs=in_specs, out_specs=out_specs, check_vma=False
    )
```

profile of v0, /device:TPU:1, one launch (start us, length us, event | category | flops | bytes accessed | tf_op | source)
XLA Modules:
  0.0 1231.6 jit_solution(22407907196482997)
XLA Ops:
  6.5 0.0 copy-start
  6.5 0.0 all-reduce.6.cloned.1.call-start
  6.5 2.2 fusion.4
  8.8 0.0 copy-done
  8.8 2.6 fusion.5
  11.4 0.0 all-reduce.6.cloned.1.call-update
  11.4 0.0 all-reduce.4.cloned.1.call-start
  11.5 1092.6 %all-reduce.6.cloned.1.call-done = (f32[512,512]{1,0:T(8,128)}, f32[1024,512]{1,0:T(8,128)}) async-done(((f32[512,512]{1,0:T(8,128)}, f32[1024,512]{1,0:T(8,128)}), (f32[512,512]{1,0:T(8,128)}, f32[1024,512]{1,0:T(8,128)})) %all-reduce.6.cloned.1.call-update) | async-done | bytes 3145744 | tf_op jit(solution)/shard_map/psum | solution.py:19
  1104.1 0.0 copy-start.1
  1104.1 2.6 convolution_bitcast_fusion
  1106.7 0.0 all-reduce.4.cloned.1.call-update
  1106.8 116.2 %all-reduce.4.cloned.1.call-done = f32[64,512]{1,0:T(8,128)} async-done(((f32[64,512]{1,0:T(8,128)}), f32[64,512]{1,0:T(8,128)}) %all-reduce.4.cloned.1.call-update) | async-done | bytes 131088 | tf_op jit(solution)/shard_map/psum | solution.py:25
  1222.9 0.0 copy-done.1
  1222.9 1.8 fusion
Async XLA Ops:
  6.5 2.2 copy-start
  6.5 1097.6 %all-reduce.6.cloned.1.call-start = ((), (), s32[]{:S(2)}) async-start(), calls=%async_computation.1 | async-start | bytes 6291456 | tf_op jit(solution)/shard_map/psum | solution.py:19
  11.4 1211.5 %all-reduce.4.cloned.1.call-start = ((), (), s32[]{:S(2)}) async-start(), calls=%async_computation | async-start | bytes 262144 | tf_op jit(solution)/shard_map/psum | solution.py:25
  1104.1 118.8 %copy-start.1 = (f32[512,512]{1,0:T(8,128)S(1)}, f32[512,512]{1,0:T(8,128)}, u32[]{:S(2)}) copy-start(f32[512,512]{1,0:T(8,128)} %get-tuple-element.5) | copy-start | bytes 3145732
Sparse Core Ops, SparseCore 0:
  11.5 1092.5 all-reduce.5
  1107.2 115.6 all-reduce.3
where the time goes:
time: 1240 us; the launch traced here: 1230 us
  waiting for transfers between devices  1210 us (98%)
  between operations  13.4 us (1%)
    psum x1, waiting for transfers between devices, on_device(): gram = lax.psum(contract_rows(factors, factors), 'feat')  1090 us
    psum x1, waiting for transfers between devices, on_device(): total = lax.psum(data_term, 'samp')  116 us
  transfers between devices with their start and end apart: 2, of which 2 were waited for; matrix products, arithmetic and copies ran while one was open for 0% of the time, Pallas kernels for 0%

commit v1 on v0

v1 whole, which is shorter than its diff:
```python
import functools

import jax
import jax.numpy as jnp
from jax import lax
from jax.experimental import pallas as pl
from jax.experimental.pallas import tpu as pltpu
from jax.sharding import PartitionSpec as P

MESH = pl.DeviceIdType.MESH
CHUNKS = ((0, 256, "x"), (256, 256, "y"), (512, 256, "x"), (768, 256, "y"), (1024, 128, "x"))
COLS = 1152
GRAM = len(CHUNKS) - 1


def contract_rows(left, right):
    return lax.dot_general(
        left, right, (((0,), (0,)), ((), ())), preferred_element_type=jnp.float32
    )


def contract_cols(left, right):
    return lax.dot_general(
        left, right, (((1,), (1,)), ((), ())), preferred_element_type=jnp.float32
    )


def kernel(sample_total, x_ref, f_ref, o_ref, xc, fc, *refs):
    n = len(CHUNKS)
    part, got1, half, got2, whole, gotz, sq = (refs[i * n:(i + 1) * n] for i in range(7))
    rows_out, rows_in, pair_send, pair_recv, send, recv, out_send, out_recv = refs[7 * n:]
    feat, samp = lax.axis_index("feat"), lax.axis_index("samp")
    core = lax.rem(feat, 2)
    at = {"y": lax.rem(lax.div(feat, 2), 4), "x": lax.rem(lax.div(feat, 8), 4)}
    stride = {"y": 2, "x": 8}

    def along(axis, step):
        there = lax.rem(at[axis] + step, 4)
        return there, (feat + (there - at[axis]) * stride[axis], samp)

    other_core = feat + 1 - 2 * core
    far = (lax.rem(feat + 32, 64), samp)
    pair = (other_core, samp)

    def row_owner(step, same):
        there = lax.rem(samp + step, 8)
        return there, (feat if same else other_core, there)

    barrier = pltpu.get_barrier_semaphore()
    partners = [along(axis, step)[1] for axis in "xy" for step in (1, 2, 3)] + [far, pair]
    partners += [row_owner(step, same)[1] for step in range(1, 8) for same in (True, False)]
    for device in partners:
        pl.semaphore_signal(barrier, inc=1, device_id=device, device_id_type=MESH)
    xc[0:64, 0:1024] = x_ref[...]
    fc[0:64, :] = f_ref[...]
    pl.semaphore_wait(barrier, len(partners))

    started = []

    def start(src, dst, send_sem, recv_sem, device):
        copy = pltpu.make_async_remote_copy(
            src_ref=src, dst_ref=dst, send_sem=send_sem, recv_sem=recv_sem,
            device_id=device, device_id_type=MESH,
        )
        copy.start()
        started.append(copy)
        return copy

    pf = start(f_ref, fc.at[64:128], pair_send.at[0], pair_recv.at[0], pair)
    px = start(x_ref, xc.at[64:128, 0:1024], pair_send.at[1], pair_recv.at[1], pair)
    pf.wait_recv()
    column = lax.broadcasted_iota(jnp.int32, (512, 128), 1)
    chosen = samp * 64 + jnp.where(column >= 64, column - 64, column)
    pick = (lax.broadcasted_iota(jnp.int32, (512, 128), 0) == chosen).astype(jnp.bfloat16)
    own_columns = jnp.dot(fc[...], pick, preferred_element_type=jnp.float32)
    xc[:, 1024:COLS] = own_columns.astype(jnp.bfloat16)
    ranks = fc[:, pl.ds(pl.multiple_of(core * 256, 256), 256)]
    px.wait_recv()

    copies = {}
    for c, (first, width, a) in enumerate(CHUNKS):
        block = contract_rows(ranks, xc[:, first:first + width])
        part[c][...] = block.reshape(4, 4, 16, width)
        for step in (1, 2, 3):
            there, device = along(a, step)
            copies[c, 0, step] = start(
                part[c].at[there], got1[c].at[step - 1],
                send.at[c, 0, step - 1], recv.at[c, 0, step - 1], device,
            )
    for c, (first, width, a) in enumerate(CHUNKS):
        b = "y" if a == "x" else "x"
        for step in (1, 2, 3):
            copies[c, 0, step].wait_recv()
        half[c][...] = (part[c][at[a]] + got1[c][0]) + (got1[c][1] + got1[c][2])
        for step in (1, 2, 3):
            there, device = along(b, step)
            copies[c, 1, step] = start(
                half[c].at[there], got2[c].at[step - 1],
                send.at[c, 1, step - 1], recv.at[c, 1, step - 1], device,
            )
    for c, (first, width, a) in enumerate(CHUNKS):
        b = "y" if a == "x" else "x"
        for step in (1, 2, 3):
            copies[c, 1, step].wait_recv()
        whole[c][...] = (half[c][at[b]] + got2[c][0]) + (got2[c][1] + got2[c][2])
        copies[c, 2] = start(whole[c], gotz[c], send.at[c, 2, 0], recv.at[c, 2, 0], far)
    for c, (first, width, a) in enumerate(CHUNKS):
        b = "y" if a == "x" else "x"
        copies[c, 2].wait_recv()
        proj = whole[c][...] + gotz[c][...]
        squared = proj * proj
        high = squared.astype(jnp.bfloat16)
        if c == GRAM:
            low = (squared - high.astype(jnp.float32)).astype(jnp.bfloat16)
            lane = lax.broadcasted_iota(jnp.int32, squared.shape, 1)
            high = jnp.where(lane >= 64, low.astype(jnp.float32), high.astype(jnp.float32))
            high = high.astype(jnp.bfloat16)
        sq[c][at[a], at[b]] = high
        for step in (1, 2, 3):
            there, device = along(b, step)
            copies[c, 3, step] = start(
                sq[c].at[at[a], at[b]], sq[c].at[at[a], at[b]],
                send.at[c, 3, step - 1], recv.at[c, 3, step - 1], device,
            )
    for c, (first, width, a) in enumerate(CHUNKS):
        for step in (1, 2, 3):
            copies[c, 3, step].wait_recv()
        for step in (1, 2, 3):
            there, device = along(a, step)
            copies[c, 4, step] = start(
                sq[c].at[at[a]], sq[c].at[at[a]],
                send.at[c, 4, step - 1], recv.at[c, 4, step - 1], device,
            )
    total = None
    for c, (first, width, a) in enumerate(CHUNKS):
        for step in (1, 2, 3):
            copies[c, 4, step].wait_recv()
        term = contract_cols(xc[:, first:first + width], sq[c][...].reshape(256, width))
        term = term * (6.0 if c == GRAM else -6.0 / sample_total)
        total = term if total is None else total + term
    rows_out[...] = total.reshape(16, 8, 256)
    done = []
    for same in (True, False):
        for step in range(8):
            slot = step + (0 if same else 8)
            there, device = row_owner(step, same)
            if slot:
                done.append(start(
                    rows_out.at[there + (0 if same else 8)], rows_in.at[slot],
                    out_send.at[slot], out_recv.at[slot], device,
                ))
    for copy in done:
        copy.wait_recv()
    own = rows_out[samp]
    for slot in range(1, 8):
        own = own + rows_in[slot]
    rest = rows_in[8]
    for slot in range(9, 16):
        rest = rest + rows_in[slot]
    o_ref[:, pl.ds(pl.multiple_of(core * 256, 256), 256)] = own
    o_ref[:, pl.ds(pl.multiple_of(256 - core * 256, 256), 256)] = rest
    for copy in started:
        copy.wait_send()


def on_device(samples, factors):
    sample_total = samples.shape[1] * lax.axis_size("samp")
    widths = [width for _, width, _ in CHUNKS]
    n = len(CHUNKS)
    scratch = [pltpu.VMEM((128, COLS), jnp.bfloat16), pltpu.VMEM((128, 512), jnp.bfloat16)]
    scratch += [pltpu.VMEM((4, 4, 16, w), jnp.float32) for w in widths]
    scratch += [pltpu.VMEM((3, 4, 16, w), jnp.float32) for w in widths]
    scratch += [pltpu.VMEM((4, 16, w), jnp.float32) for w in widths]
    scratch += [pltpu.VMEM((3, 16, w), jnp.float32) for w in widths]
    scratch += [pltpu.VMEM((16, w), jnp.float32) for w in widths]
    scratch += [pltpu.VMEM((16, w), jnp.float32) for w in widths]
    scratch += [pltpu.VMEM((4, 4, 16, w), jnp.bfloat16) for w in widths]
    scratch += [pltpu.VMEM((16, 8, 256), jnp.float32), pltpu.VMEM((16, 8, 256), jnp.float32)]
    scratch += [pltpu.SemaphoreType.DMA((2,)), pltpu.SemaphoreType.DMA((2,))]
    scratch += [pltpu.SemaphoreType.DMA((n, 5, 3)), pltpu.SemaphoreType.DMA((n, 5, 3))]
    scratch += [pltpu.SemaphoreType.DMA((16,)), pltpu.SemaphoreType.DMA((16,))]
    return pl.pallas_call(
        functools.partial(kernel, sample_total),
        out_shape=jax.ShapeDtypeStruct((8, 512), jnp.float32),
        in_specs=[pl.BlockSpec(memory_space=pltpu.VMEM)] * 2,
        out_specs=pl.BlockSpec(memory_space=pltpu.VMEM),
        scratch_shapes=scratch,
        compiler_params=pltpu.CompilerParams(
            collective_id=0, has_side_effects=True, vmem_limit_bytes=32 * 2**20
        ),
        cost_estimate=pl.CostEstimate(
            flops=2 * 128 * COLS * 256 * 2, bytes_accessed=1 << 20, transcendentals=0
        ),
    )(samples, factors)


def solution(mesh):
    in_specs = (P("feat", "samp"), P("feat", None))
    out_specs = P(("feat", "samp"), None)
    return jax.shard_map(
        on_device, mesh=mesh, in_specs=in_specs, out_specs=out_specs, check_vma=False
    )
```

time: 1240 us -> 59.4 us (0.05)
  waiting for transfers between devices: 1210 us -> 0 us
  Pallas kernels: 0 us -> 56.9 us
  between operations: 13.4 us -> 0.01 us
    psum x2 -> x0, waiting for transfers between devices: 1210 us -> none  [the longest x1 1090 us: on_device(): gram = lax.psum(contract_rows(factors, factors), 'feat')]
    pallas_call x0 -> x1, Pallas kernels: none -> 56.9 us  [on_device(): pl.pallas_call(functools.partial(kernel, sample_total), out_shape=jax.Sha...]
  transfers between devices with their start and end apart: 2 -> 0, of which waited for: 2 -> 0; matrix products, arithmetic and copies ran while one was open for 0% -> 0% of each run, Pallas kernels for 0% -> 0%
where the time goes in v1:
time: 59.4 us; the launch traced here: 59.3 us
  Pallas kernels  56.9 us (96%)
  local copies, waits for them, and re-layouts  2.35 us (4%)
    pallas_call x1, Pallas kernels, on_device(): pl.pallas_call(functools.partial(kernel, sample_total), out_shape=jax.Sha...  56.9 us
    unnamed x5, local copies, waits for them, and re-layouts  2.35 us

profile of v1, /device:TPU:1, one launch (start us, length us, event | category | flops | bytes accessed | tf_op | source)
XLA Modules:
  0.0 59.3 jit_solution(10481372809518750779)
XLA Ops:
  0.0 0.0 copy-start
  0.0 0.9 %copy-done = bf16[64,1024]{1,0:T(8,128)(2,1)S(1)} copy-done((bf16[64,1024]{1,0:T(8,128)(2,1)S(1)}, bf16[64,1024]{1,0:T(8,128)(2,1)}, u32[]{:S(2)}) %copy-start) | copy-done | bytes 131096
  0.9 0.0 copy-start.1
  0.9 0.8 %copy-done.1 = bf16[64,512]{1,0:T(8,128)(2,1)S(1)} copy-done((bf16[64,512]{1,0:T(8,128)(2,1)S(1)}, bf16[64,512]{1,0:T(8,128)(2,1)}, u32[]{:S(2)}) %copy-start.1) | copy-done | bytes 65560
  1.7 56.9 %shard_map.28 = f32[8,512]{1,0:T(8,128)S(1)} custom-call(bf16[64,1024]{1,0:T(8,128)(2,1)S(1)} %copy-done, bf16[64,512]{1,0:T(8,128)(2,1)S(1)} %copy-done.1), custom_call_target="tpu_custom_call" | custom-call | flops 150994944 | bytes 1048576 | tf_op jit(solution)/shard_map/pallas_call | solution.py:182
  58.6 0.6 %copy.4 = f32[8,512]{1,0:T(8,128)} copy(f32[8,512]{1,0:T(8,128)S(1)} %shard_map.28) | data formatting | bytes 32768
Async XLA Ops:
  0.0 0.9 %copy-start = (bf16[64,1024]{1,0:T(8,128)(2,1)S(1)}, bf16[64,1024]{1,0:T(8,128)(2,1)}, u32[]{:S(2)}) copy-start(bf16[64,1024]{1,0:T(8,128)(2,1)} %x_ref.1) | copy-start | bytes 393220
  0.9 0.8 %copy-start.1 = (bf16[64,512]{1,0:T(8,128)(2,1)S(1)}, bf16[64,512]{1,0:T(8,128)(2,1)}, u32[]{:S(2)}) copy-start(bf16[64,512]{1,0:T(8,128)(2,1)} %f_ref.1) | copy-start | bytes 196612

commit v2 on v0

v2 whole, which is shorter than its diff:
```python
import functools

import jax
import jax.numpy as jnp
from jax import lax
from jax.experimental import pallas as pl
from jax.experimental.pallas import tpu as pltpu
from jax.sharding import PartitionSpec as P

MESH = pl.DeviceIdType.MESH
SIDES = (("y", "x"), ("x", "y"))
CHUNKS = ((0, 0, 256, 256), (1, 512, 256, 256), (0, 256, 256, 384), (1, 768, 256, 256))
EARLY, LATE = (0, 1), (2, 3)
GRAM = 2


def contract_rows(left, right):
    return lax.dot_general(
        left, right, (((0,), (0,)), ((), ())), preferred_element_type=jnp.float32
    )


def contract_cols(left, right):
    return lax.dot_general(
        left, right, (((1,), (1,)), ((), ())), preferred_element_type=jnp.float32
    )


def kernel(sample_total, x_ref, f_ref, o_ref, fv, *refs):
    n = len(CHUNKS)
    xs, part, gotp, half, gotr, whole, gotz, sq = (refs[n * i:n * (i + 1)] for i in range(8))
    fs, dout, din = (refs[8 * n + 2 * i:8 * n + 2 * i + 2] for i in range(3))
    rows_out, rows_in, here, local_sem, f_send, f_recv, d_send, d_recv, send, recv, out_send, out_recv = refs[8 * n + 6:]
    feat, samp = lax.axis_index("feat"), lax.axis_index("samp")
    core = lax.rem(feat, 2)
    at = {"y": lax.rem(lax.div(feat, 2), 4), "x": lax.rem(lax.div(feat, 8), 4)}
    stride = {"y": 2, "x": 8}

    def along(axis, step, device=feat):
        there = lax.rem(at[axis] + step, 4)
        return there, (device + (there - at[axis]) * stride[axis], samp)

    other_core = feat + 1 - 2 * core
    far = (lax.rem(feat + 32, 64), samp)
    pair = (other_core, samp)

    def beside(step):
        z = lax.rem(lax.div(feat, 32) * 8 + samp + step + 16, 16)
        return (lax.rem(feat, 32) + 32 * lax.div(z, 8), lax.rem(z, 8))

    def row_owner(step):
        there = lax.rem(samp + step, 8)
        return there, (feat, there)

    barrier = pltpu.get_barrier_semaphore()
    partners = [along(axis, step, device)[1] for step in (2, 1, 3) for axis in "xy" for device in (feat, other_core)]
    partners += [pair, beside(1), beside(-1)]
    for device in partners:
        pl.semaphore_signal(barrier, inc=1, device_id=device, device_id_type=MESH)
    loads = [pltpu.make_async_copy(f_ref, fv, local_sem.at[n])]
    for c, (s, first, count, width) in enumerate(CHUNKS):
        loads.append(pltpu.make_async_copy(
            x_ref.at[:, first:first + count], xs[c].at[at[SIDES[s][0]], :, 0:count], local_sem.at[c]
        ))
    for load in loads:
        load.start()
    column = lax.broadcasted_iota(jnp.int32, (512, 128), 1)
    chosen = samp * 64 + jnp.where(column >= 64, column - 64, column)
    pick = (lax.broadcasted_iota(jnp.int32, (512, 128), 0) == chosen).astype(jnp.bfloat16)
    loads[0].wait()
    own_columns = jnp.dot(fv[...], pick, preferred_element_type=jnp.float32)
    xs[GRAM][at[SIDES[0][0]], :, 256:384] = own_columns.astype(jnp.bfloat16)
    for s, (g, r) in enumerate(SIDES):
        fs[s][at[g]] = fv[:, pl.ds(pl.multiple_of(at[g] * 128, 128), 128)]
    for load in loads[1:]:
        load.wait()
    pl.semaphore_wait(barrier, len(partners))

    def tell(step):
        for device in (beside(step), beside(-step)):
            pl.semaphore_signal(here.at[step // 2], inc=1, device_id=device, device_id_type=MESH)

    def hear(step):
        pl.semaphore_wait(here.at[step // 2], 2)

    started = []

    def start(src, dst, send_sem, recv_sem, device):
        copy = pltpu.make_async_remote_copy(
            src_ref=src, dst_ref=dst, send_sem=send_sem, recv_sem=recv_sem,
            device_id=device, device_id_type=MESH,
        )
        copy.start()
        started.append(copy)
        return copy

    copies = {}
    for step in (2, 1, 3):
        for s, (g, r) in enumerate(SIDES):
            there, device = along(g, step)
            lanes = pl.ds(pl.multiple_of(there * 128, 128), 128)
            copies["f", s, step] = start(
                fv.at[:, lanes], fs[s].at[at[g]], f_send.at[s, step], f_recv.at[s, step], device
            )
    for group in (EARLY, LATE):
        if group is LATE:
            tell(1)
        for step in (2, 1, 3):
            for c in group:
                g = SIDES[CHUNKS[c][0]][0]
                there, device = along(g, step)
                copies[c, 0, step] = start(
                    xs[c].at[at[g]], xs[c].at[at[g]], send.at[c, 0, step], recv.at[c, 0, step], device
                )

    weights = []
    for s in range(2):
        for step in (1, 3, 2):
            copies["f", s, step].wait_recv()
        weights.append(jnp.transpose(fs[s][...].reshape(256, 128)))

    hear(1)
    tell(2)

    def project(c):
        s, first, count, width = CHUNKS[c]
        for step in (1, 3, 2):
            copies[c, 0, step].wait_recv()
        block = jnp.dot(weights[s], xs[c][...].reshape(256, width), preferred_element_type=jnp.float32)
        part[c][...] = block.reshape(2, 4, 16, width)
        copies[c, 1] = start(part[c].at[1 - core], gotp[c], send.at[c, 1, 0], recv.at[c, 1, 0], pair)

    def scatter(c):
        r = SIDES[CHUNKS[c][0]][1]
        copies[c, 1].wait_recv()
        half[c][...] = part[c][core] + gotp[c][...]
        for step in (2, 1, 3):
            there, device = along(r, step)
            copies[c, 2, step] = start(
                half[c].at[there], gotr[c].at[step - 1], send.at[c, 2, step], recv.at[c, 2, step], device
            )

    def exchange(c):
        r = SIDES[CHUNKS[c][0]][1]
        for step in (1, 3, 2):
            copies[c, 2, step].wait_recv()
        whole[c][...] = (half[c][at[r]] + gotr[c][0]) + (gotr[c][1] + gotr[c][2])
        copies[c, 3] = start(whole[c], gotz[c], send.at[c, 3, 0], recv.at[c, 3, 0], far)

    def square(c):
        r = SIDES[CHUNKS[c][0]][1]
        copies[c, 3].wait_recv()
        proj = whole[c][...] + gotz[c][...]
        squared = proj * proj
        high = squared.astype(jnp.bfloat16)
        own = sq[c].at[core, at[r]]
        if c == GRAM:
            own[:, 0:256] = high[:, 0:256]
            exact, wide = squared[:, 256:], high[:, 256:].astype(jnp.float32)
            lane = lax.broadcasted_iota(jnp.int32, exact.shape, 1)
            own[:, 256:] = jnp.where(lane >= 64, exact - wide, wide).astype(jnp.bfloat16)
        else:
            own[...] = high
        for step in (2, 1, 3):
            for stage, core_there in ((4, feat), (5, other_core)):
                there, device = along(r, step, core_there)
                copies[c, stage, step] = start(own, own, send.at[c, stage, step], recv.at[c, stage, step], device)
        copies[c, 5, 0] = start(own, own, send.at[c, 5, 0], recv.at[c, 5, 0], pair)

    def term(c):
        s, first, count, width = CHUNKS[c]
        copies[c, 5, 0].wait_recv()
        for step in (1, 3, 2):
            copies[c, 4, step].wait_recv()
            copies[c, 5, step].wait_recv()
        left, right = xs[c][...].reshape(256, width), sq[c][...].reshape(128, width)
        product = (-6.0 / sample_total) * contract_cols(left[:, 0:count], right[:, 0:count])
        if c == GRAM:
            product = product + 6.0 * contract_cols(left[:, count:], right[:, count:])
        return product

    for c in EARLY:
        project(c)
    hear(2)
    tell(4)
    for c in EARLY:
        scatter(c)
    for c in LATE:
        project(c)
    for c in LATE:
        scatter(c)
    hear(4)
    for c in EARLY + LATE:
        exchange(c)
    for c in EARLY + LATE:
        square(c)
    total = [0.0, 0.0]
    for group in (EARLY, LATE):
        for c in group:
            s = CHUNKS[c][0]
            total[s] = total[s] + term(c)
            if c in LATE:
                g = SIDES[s][0]
                dout[s][...] = total[s].reshape(4, 64, 128)
                for step in (2, 1, 3):
                    there, device = along(g, step)
                    copies["d", s, step] = start(
                        dout[s].at[there], din[s].at[at[g]], d_send.at[s, step], d_recv.at[s, step], device
                    )
                din[s][at[g]] = dout[s][at[g]]
    for step in (1, 3, 2):
        for s in range(2):
            copies["d", s, step].wait_recv()
    for chunk in range(4):
        rows_out[:, chunk] = (din[0][chunk] + din[1][chunk]).reshape(8, 8, 128)
    done = []
    for step in (4, 3, 5, 2, 6, 1, 7):
        there, device = row_owner(step)
        done.append(start(
            rows_out.at[there], rows_in.at[step - 1],
            out_send.at[step - 1], out_recv.at[step - 1], device,
        ))
    for copy in started[:-7]:
        copy.wait_send()
    for copy in done:
        copy.wait_recv()
    own = rows_out[samp]
    for slot in range(7):
        own = own + rows_in[slot]
    for chunk in range(4):
        o_ref[:, chunk * 128:(chunk + 1) * 128] = own[chunk]
    for copy in done:
        copy.wait_send()


def on_device(samples, factors):
    sample_total = samples.shape[1] * lax.axis_size("samp")
    n = len(CHUNKS)

    def each(shape, dtype):
        return [pltpu.VMEM(shape + (width,), dtype) for _, _, _, width in CHUNKS]

    scratch = [pltpu.VMEM((64, 512), jnp.bfloat16)]
    scratch += each((4, 64), jnp.bfloat16)
    scratch += each((2, 4, 16), jnp.float32)
    scratch += each((4, 16), jnp.float32)
    scratch += each((4, 16), jnp.float32)
    scratch += each((3, 16), jnp.float32)
    scratch += each((16,), jnp.float32)
    scratch += each((16,), jnp.float32)
    scratch += each((2, 4, 16), jnp.bfloat16)
    scratch += [pltpu.VMEM((4, 64, 128), jnp.bfloat16)] * 2
    scratch += [pltpu.VMEM((4, 64, 128), jnp.float32)] * 4
    scratch += [pltpu.VMEM((8, 4, 8, 128), jnp.float32), pltpu.VMEM((7, 4, 8, 128), jnp.float32)]
    scratch += [pltpu.SemaphoreType.REGULAR((3,)), pltpu.SemaphoreType.DMA((n + 1,))]
    scratch += [pltpu.SemaphoreType.DMA((2, 4))] * 4
    scratch += [pltpu.SemaphoreType.DMA((n, 6, 4)), pltpu.SemaphoreType.DMA((n, 6, 4))]
    scratch += [pltpu.SemaphoreType.DMA((7,)), pltpu.SemaphoreType.DMA((7,))]
    return pl.pallas_call(
        functools.partial(kernel, sample_total),
        out_shape=pltpu.VMEM((8, 512), jnp.float32),
        in_specs=[pl.BlockSpec(memory_space=pltpu.HBM)] * 2,
        out_specs=pl.BlockSpec(memory_space=pltpu.VMEM),
        scratch_shapes=scratch,
        compiler_params=pltpu.CompilerParams(
            collective_id=0, has_side_effects=True, vmem_limit_bytes=32 * 2**20
        ),
        cost_estimate=pl.CostEstimate(
            flops=4 * 256 * 128 * 1152, bytes_accessed=1 << 20, transcendentals=0
        ),
    )(
        pltpu.with_memory_space_constraint(samples, pltpu.HBM),
        pltpu.with_memory_space_constraint(factors, pltpu.HBM),
    )


def solution(mesh):
    in_specs = (P("feat", "samp"), P("feat", None))
    out_specs = P(("feat", "samp"), None)
    return jax.shard_map(
        on_device, mesh=mesh, in_specs=in_specs, out_specs=out_specs, check_vma=False
    )
```

time: 1240 us -> 53.8 us (0.04)
  waiting for transfers between devices: 1210 us -> 0 us
  Pallas kernels: 0 us -> 53.1 us
  between operations: 13.4 us -> 0.01 us
    psum x2 -> x0, waiting for transfers between devices: 1210 us -> none  [the longest x1 1090 us: on_device(): gram = lax.psum(contract_rows(factors, factors), 'feat')]
    pallas_call x0 -> x1, Pallas kernels: none -> 53.1 us  [on_device(): pl.pallas_call(functools.partial(kernel, sample_total), out_shape=pltpu.V...]
  transfers between devices with their start and end apart: 2 -> 0, of which waited for: 2 -> 0; matrix products, arithmetic and copies ran while one was open for 0% -> 0% of each run, Pallas kernels for 0% -> 0%
where the time goes in v2:
time: 53.8 us; the launch traced here: 53.7 us
  Pallas kernels  53.1 us (99%)
  local copies, waits for them, and re-layouts  0.61 us (1%)
    pallas_call x1, Pallas kernels, on_device(): pl.pallas_call(functools.partial(kernel, sample_total), out_shape=pltpu.V...  53.1 us

profile of v2, /device:TPU:1, one launch (start us, length us, event | category | flops | bytes accessed | tf_op | source)
XLA Modules:
  0.0 53.7 jit_solution(14665925233019094230)
XLA Ops:
  0.0 53.1 %shard_map.28 = f32[8,512]{1,0:T(8,128)S(1)} custom-call(bf16[64,1024]{1,0:T(8,128)(2,1)} %x_ref.1, bf16[64,512]{1,0:T(8,128)(2,1)} %f_ref.1), custom_call_target="tpu_custom_call" | custom-call | flops 150994944 | bytes 1048576 | tf_op jit(solution)/shard_map/pallas_call | solution.py:259
  53.1 0.6 %copy.4 = f32[8,512]{1,0:T(8,128)} copy(f32[8,512]{1,0:T(8,128)S(1)} %shard_map.28) | data formatting | bytes 32768

commit v3 on v2

--- a/solution.py
+++ b/solution.py
@@ -9,9 +9,9 @@
 
 MESH = pl.DeviceIdType.MESH
 SIDES = (("y", "x"), ("x", "y"))
-CHUNKS = ((0, 0, 256, 256), (1, 512, 256, 256), (0, 256, 256, 384), (1, 768, 256, 256))
-EARLY, LATE = (0, 1), (2, 3)
-GRAM = 2
+CHUNKS = ((0, 0, 384, 384), (1, 512, 256, 256), (0, 384, 128, 256), (1, 768, 256, 256))
+GROUPS = ((0, 1), (2, 3))
+GRAM, LAST = 2, GROUPS[-1]
 
 
 def contract_rows(left, right):
@@ -28,9 +28,9 @@
 
 def kernel(sample_total, x_ref, f_ref, o_ref, fv, *refs):
     n = len(CHUNKS)
-    xs, part, gotp, half, gotr, whole, gotz, sq = (refs[n * i:n * (i + 1)] for i in range(8))
-    fs, dout, din = (refs[8 * n + 2 * i:8 * n + 2 * i + 2] for i in range(3))
-    rows_out, rows_in, here, local_sem, f_send, f_recv, d_send, d_recv, send, recv, out_send, out_recv = refs[8 * n + 6:]
+    xs, part, gotp, gotr, whole, gotz, sq = (refs[n * i:n * (i + 1)] for i in range(7))
+    fs, dout, din = (refs[7 * n + 2 * i:7 * n + 2 * i + 2] for i in range(3))
+    rows_out, rows_in, here, local_sem, f_send, f_recv, d_send, d_recv, send, recv, out_send, out_recv = refs[7 * n + 6:]
     feat, samp = lax.axis_index("feat"), lax.axis_index("samp")
     core = lax.rem(feat, 2)
     at = {"y": lax.rem(lax.div(feat, 2), 4), "x": lax.rem(lax.div(feat, 8), 4)}
@@ -64,14 +64,7 @@
         ))
     for load in loads:
         load.start()
-    column = lax.broadcasted_iota(jnp.int32, (512, 128), 1)
-    chosen = samp * 64 + jnp.where(column >= 64, column - 64, column)
-    pick = (lax.broadcasted_iota(jnp.int32, (512, 128), 0) == chosen).astype(jnp.bfloat16)
     loads[0].wait()
-    own_columns = jnp.dot(fv[...], pick, preferred_element_type=jnp.float32)
-    xs[GRAM][at[SIDES[0][0]], :, 256:384] = own_columns.astype(jnp.bfloat16)
-    for s, (g, r) in enumerate(SIDES):
-        fs[s][at[g]] = fv[:, pl.ds(pl.multiple_of(at[g] * 128, 128), 128)]
     for load in loads[1:]:
         load.wait()
     pl.semaphore_wait(barrier, len(partners))
@@ -83,6 +76,7 @@
     def hear(step):
         pl.semaphore_wait(here.at[step // 2], 2)
 
+    tell(1)
     started = []
 
     def start(src, dst, send_sem, recv_sem, device):
@@ -102,9 +96,13 @@
             copies["f", s, step] = start(
                 fv.at[:, lanes], fs[s].at[at[g]], f_send.at[s, step], f_recv.at[s, step], device
             )
-    for group in (EARLY, LATE):
-        if group is LATE:
-            tell(1)
+    for group in GROUPS:
+        if GRAM in group:
+            column = lax.broadcasted_iota(jnp.int32, (512, 128), 1)
+            chosen = samp * 64 + jnp.where(column >= 64, column - 64, column)
+            pick = (lax.broadcasted_iota(jnp.int32, (512, 128), 0) == chosen).astype(jnp.bfloat16)
+            own_columns = jnp.dot(fv[...], pick, preferred_element_type=jnp.float32)
+            xs[GRAM][at[SIDES[0][0]], :, CHUNKS[GRAM][2]:] = own_columns.astype(jnp.bfloat16)
         for step in (2, 1, 3):
             for c in group:
                 g = SIDES[CHUNKS[c][0]][0]
@@ -113,14 +111,18 @@
                     xs[c].at[at[g]], xs[c].at[at[g]], send.at[c, 0, step], recv.at[c, 0, step], device
                 )
 
+    for s, (g, r) in enumerate(SIDES):
+        fs[s][at[g]] = fv[:, pl.ds(pl.multiple_of(at[g] * 128, 128), 128)]
+    hear(1)
+    tell(2)
     weights = []
     for s in range(2):
         for step in (1, 3, 2):
             copies["f", s, step].wait_recv()
         weights.append(jnp.transpose(fs[s][...].reshape(256, 128)))
 
-    hear(1)
-    tell(2)
+    hear(2)
+    tell(4)
 
     def project(c):
         s, first, count, width = CHUNKS[c]
@@ -128,37 +130,38 @@
             copies[c, 0, step].wait_recv()
         block = jnp.dot(weights[s], xs[c][...].reshape(256, width), preferred_element_type=jnp.float32)
         part[c][...] = block.reshape(2, 4, 16, width)
-        copies[c, 1] = start(part[c].at[1 - core], gotp[c], send.at[c, 1, 0], recv.at[c, 1, 0], pair)
-
-    def scatter(c):
-        r = SIDES[CHUNKS[c][0]][1]
-        copies[c, 1].wait_recv()
-        half[c][...] = part[c][core] + gotp[c][...]
+        r = SIDES[s][1]
+        copies[c, 1, 0] = start(part[c].at[1 - core, at[r]], gotp[c].at[0], send.at[c, 1, 0], recv.at[c, 1, 0], pair)
         for step in (2, 1, 3):
-            there, device = along(r, step)
-            copies[c, 2, step] = start(
-                half[c].at[there], gotr[c].at[step - 1], send.at[c, 2, step], recv.at[c, 2, step], device
-            )
+            for stage, device, there_core in ((1, other_core, 1 - core), (2, feat, core)):
+                there, device = along(r, step, device)
+                copies[c, stage, step] = start(
+                    part[c].at[there_core, there], (gotp if stage == 1 else gotr)[c].at[step - (stage == 2)],
+                    send.at[c, stage, step], recv.at[c, stage, step], device,
+                )
 
     def exchange(c):
         r = SIDES[CHUNKS[c][0]][1]
         for step in (1, 3, 2):
             copies[c, 2, step].wait_recv()
-        whole[c][...] = (half[c][at[r]] + gotr[c][0]) + (gotr[c][1] + gotr[c][2])
+            copies[c, 1, step].wait_recv()
+        copies[c, 1, 0].wait_recv()
+        same = (part[c][core, at[r]] + gotr[c][0]) + (gotr[c][1] + gotr[c][2])
+        whole[c][...] = same + ((gotp[c][0] + gotp[c][1]) + (gotp[c][2] + gotp[c][3]))
         copies[c, 3] = start(whole[c], gotz[c], send.at[c, 3, 0], recv.at[c, 3, 0], far)
 
     def square(c):
-        r = SIDES[CHUNKS[c][0]][1]
+        r, count = SIDES[CHUNKS[c][0]][1], CHUNKS[c][2]
         copies[c, 3].wait_recv()
         proj = whole[c][...] + gotz[c][...]
         squared = proj * proj
         high = squared.astype(jnp.bfloat16)
         own = sq[c].at[core, at[r]]
         if c == GRAM:
-            own[:, 0:256] = high[:, 0:256]
-            exact, wide = squared[:, 256:], high[:, 256:].astype(jnp.float32)
+            own[:, 0:count] = high[:, 0:count]
+            exact, wide = squared[:, count:], high[:, count:].astype(jnp.float32)
             lane = lax.broadcasted_iota(jnp.int32, exact.shape, 1)
-            own[:, 256:] = jnp.where(lane >= 64, exact - wide, wide).astype(jnp.bfloat16)
+            own[:, count:] = jnp.where(lane >= 64, exact - wide, wide).astype(jnp.bfloat16)
         else:
             own[...] = high
         for step in (2, 1, 3):
@@ -179,27 +182,25 @@
             product = product + 6.0 * contract_cols(left[:, count:], right[:, count:])
         return product
 
-    for c in EARLY:
-        project(c)
-    hear(2)
-    tell(4)
-    for c in EARLY:
-        scatter(c)
-    for c in LATE:
-        project(c)
-    for c in LATE:
-        scatter(c)
-    hear(4)
-    for c in EARLY + LATE:
+    for k, group in enumerate(GROUPS):
+        for c in group:
+            project(c)
+        if k == 1:
+            hear(4)
+        if k:
+            for c in GROUPS[k - 1]:
+                exchange(c)
+    for c in GROUPS[-1]:
         exchange(c)
-    for c in EARLY + LATE:
-        square(c)
+    for group in GROUPS:
+        for c in group:
+            square(c)
     total = [0.0, 0.0]
-    for group in (EARLY, LATE):
+    for group in GROUPS:
         for c in group:
             s = CHUNKS[c][0]
             total[s] = total[s] + term(c)
-            if c in LATE:
+            if c in LAST:
                 g = SIDES[s][0]
                 dout[s][...] = total[s].reshape(4, 64, 128)
                 for step in (2, 1, 3):
@@ -214,8 +215,10 @@
     for chunk in range(4):
         rows_out[:, chunk] = (din[0][chunk] + din[1][chunk]).reshape(8, 8, 128)
     done = []
-    for step in (4, 3, 5, 2, 6, 1, 7):
-        there, device = row_owner(step)
+    for order in range(7):
+        there = jnp.where(samp < 4, 7 - order - jnp.where(7 - order <= samp, 1, 0), order + jnp.where(order >= samp, 1, 0))
+        step = lax.rem(there + 8 - samp, 8)
+        device = (feat, there)
         done.append(start(
             rows_out.at[there], rows_in.at[step - 1],
             out_send.at[step - 1], out_recv.at[step - 1], device,
@@ -243,7 +246,6 @@
     scratch = [pltpu.VMEM((64, 512), jnp.bfloat16)]
     scratch += each((4, 64), jnp.bfloat16)
     scratch += each((2, 4, 16), jnp.float32)
-    scratch += each((4, 16), jnp.float32)
     scratch += each((4, 16), jnp.float32)
     scratch += each((3, 16), jnp.float32)
     scratch += each((16,), jnp.float32)

time: 53.8 us -> 52 us (0.967)
  Pallas kernels: 53.1 us -> 51.1 us
    pallas_call x1, Pallas kernels: 53.1 us -> 51.1 us  [on_device(): pl.pallas_call(functools.partial(kernel, sample_total), out_shape=pltpu.V...]
where the time goes in v3:
time: 52 us; the launch traced here: 51.7 us
  Pallas kernels  51.1 us (98%)
  local copies, waits for them, and re-layouts  0.61 us (1%)
    pallas_call x1, Pallas kernels, on_device(): pl.pallas_call(functools.partial(kernel, sample_total), out_shape=pltpu.V...  51.1 us

profile of v3, /device:TPU:1, one launch (start us, length us, event | category | flops | bytes accessed | tf_op | source)
XLA Modules:
  0.0 51.7 jit_solution(4009662902177454952)
XLA Ops:
  0.0 51.1 %shard_map.28 = f32[8,512]{1,0:T(8,128)S(1)} custom-call(bf16[64,1024]{1,0:T(8,128)(2,1)} %x_ref.1, bf16[64,512]{1,0:T(8,128)(2,1)} %f_ref.1), custom_call_target="tpu_custom_call" | custom-call | flops 150994944 | bytes 1048576 | tf_op jit(solution)/shard_map/pallas_call | solution.py:261
  51.1 0.6 %copy.4 = f32[8,512]{1,0:T(8,128)} copy(f32[8,512]{1,0:T(8,128)S(1)} %shard_map.28) | data formatting | bytes 32768

commit v4 on v3

--- a/solution.py
+++ b/solution.py
@@ -28,9 +28,9 @@
 
 def kernel(sample_total, x_ref, f_ref, o_ref, fv, *refs):
     n = len(CHUNKS)
-    xs, part, gotp, gotr, whole, gotz, sq = (refs[n * i:n * (i + 1)] for i in range(7))
-    fs, dout, din = (refs[7 * n + 2 * i:7 * n + 2 * i + 2] for i in range(3))
-    rows_out, rows_in, here, local_sem, f_send, f_recv, d_send, d_recv, send, recv, out_send, out_recv = refs[7 * n + 6:]
+    xs, part, got, whole, gotz, sq = (refs[n * i:n * (i + 1)] for i in range(6))
+    fs, dout, din = (refs[6 * n + 2 * i:6 * n + 2 * i + 2] for i in range(3))
+    rows_out, rows_in, here, local_sem, f_send, f_recv, d_send, d_recv, send, recv, out_send, out_recv = refs[6 * n + 6:]
     feat, samp = lax.axis_index("feat"), lax.axis_index("samp")
     core = lax.rem(feat, 2)
     at = {"y": lax.rem(lax.div(feat, 2), 4), "x": lax.rem(lax.div(feat, 8), 4)}
@@ -77,24 +77,21 @@
         pl.semaphore_wait(here.at[step // 2], 2)
 
     tell(1)
-    started = []
-
     def start(src, dst, send_sem, recv_sem, device):
-        copy = pltpu.make_async_remote_copy(
+        pltpu.make_async_remote_copy(
             src_ref=src, dst_ref=dst, send_sem=send_sem, recv_sem=recv_sem,
             device_id=device, device_id_type=MESH,
-        )
-        copy.start()
-        started.append(copy)
-        return copy
-
-    copies = {}
+        ).start()
+
+    def wait(ref, sem):
+        pltpu.make_async_copy(ref, ref, sem).wait()
+
     for step in (2, 1, 3):
         for s, (g, r) in enumerate(SIDES):
             there, device = along(g, step)
             lanes = pl.ds(pl.multiple_of(there * 128, 128), 128)
-            copies["f", s, step] = start(
-                fv.at[:, lanes], fs[s].at[at[g]], f_send.at[s, step], f_recv.at[s, step], device
+            start(
+                fv.at[:, lanes], fs[s].at[at[g]], f_send.at[s], f_recv.at[s], device
             )
     for group in GROUPS:
         if GRAM in group:
@@ -107,8 +104,8 @@
             for c in group:
                 g = SIDES[CHUNKS[c][0]][0]
                 there, device = along(g, step)
-                copies[c, 0, step] = start(
-                    xs[c].at[at[g]], xs[c].at[at[g]], send.at[c, 0, step], recv.at[c, 0, step], device
+                start(
+                    xs[c].at[at[g]], xs[c].at[at[g]], send.at[c, 0], recv.at[c, 0], device
                 )
 
     for s, (g, r) in enumerate(SIDES):
@@ -117,8 +114,7 @@
     tell(2)
     weights = []
     for s in range(2):
-        for step in (1, 3, 2):
-            copies["f", s, step].wait_recv()
+        wait(fs[s].at[0:3], f_recv.at[s])
         weights.append(jnp.transpose(fs[s][...].reshape(256, 128)))
 
     hear(2)
@@ -126,37 +122,33 @@
 
     def project(c):
         s, first, count, width = CHUNKS[c]
-        for step in (1, 3, 2):
-            copies[c, 0, step].wait_recv()
+        wait(xs[c].at[0:3], recv.at[c, 0])
         block = jnp.dot(weights[s], xs[c][...].reshape(256, width), preferred_element_type=jnp.float32)
         part[c][...] = block.reshape(2, 4, 16, width)
         r = SIDES[s][1]
-        copies[c, 1, 0] = start(part[c].at[1 - core, at[r]], gotp[c].at[0], send.at[c, 1, 0], recv.at[c, 1, 0], pair)
+        start(part[c].at[1 - core, at[r]], got[c].at[0], send.at[c, 1], recv.at[c, 1], pair)
         for step in (2, 1, 3):
-            for stage, device, there_core in ((1, other_core, 1 - core), (2, feat, core)):
+            for slot, device, there_core in ((step, other_core, 1 - core), (3 + step, feat, core)):
                 there, device = along(r, step, device)
-                copies[c, stage, step] = start(
-                    part[c].at[there_core, there], (gotp if stage == 1 else gotr)[c].at[step - (stage == 2)],
-                    send.at[c, stage, step], recv.at[c, stage, step], device,
+                start(
+                    part[c].at[there_core, there], got[c].at[slot], send.at[c, 1], recv.at[c, 1], device
                 )
 
     def exchange(c):
         r = SIDES[CHUNKS[c][0]][1]
-        for step in (1, 3, 2):
-            copies[c, 2, step].wait_recv()
-            copies[c, 1, step].wait_recv()
-        copies[c, 1, 0].wait_recv()
-        same = (part[c][core, at[r]] + gotr[c][0]) + (gotr[c][1] + gotr[c][2])
-        whole[c][...] = same + ((gotp[c][0] + gotp[c][1]) + (gotp[c][2] + gotp[c][3]))
-        copies[c, 3] = start(whole[c], gotz[c], send.at[c, 3, 0], recv.at[c, 3, 0], far)
+        wait(got[c], recv.at[c, 1])
+        whole[c][...] = ((part[c][core, at[r]] + got[c][0]) + (got[c][1] + got[c][2])) + (
+            (got[c][3] + got[c][4]) + (got[c][5] + got[c][6])
+        )
+        start(whole[c], gotz[c], send.at[c, 2], recv.at[c, 2], far)
 
     def square(c):
         r, count = SIDES[CHUNKS[c][0]][1], CHUNKS[c][2]
-        copies[c, 3].wait_recv()
+        wait(gotz[c], recv.at[c, 2])
         proj = whole[c][...] + gotz[c][...]
         squared = proj * proj
         high = squared.astype(jnp.bfloat16)
-        own = sq[c].at[core, at[r]]
+        own = sq[c].at[core * 4 + at[r]]
         if c == GRAM:
             own[:, 0:count] = high[:, 0:count]
             exact, wide = squared[:, count:], high[:, count:].astype(jnp.float32)
@@ -165,17 +157,14 @@
         else:
             own[...] = high
         for step in (2, 1, 3):
-            for stage, core_there in ((4, feat), (5, other_core)):
+            for core_there in (feat, other_core):
                 there, device = along(r, step, core_there)
-                copies[c, stage, step] = start(own, own, send.at[c, stage, step], recv.at[c, stage, step], device)
-        copies[c, 5, 0] = start(own, own, send.at[c, 5, 0], recv.at[c, 5, 0], pair)
+                start(own, own, send.at[c, 3], recv.at[c, 3], device)
+        start(own, own, send.at[c, 3], recv.at[c, 3], pair)
 
     def term(c):
         s, first, count, width = CHUNKS[c]
-        copies[c, 5, 0].wait_recv()
-        for step in (1, 3, 2):
-            copies[c, 4, step].wait_recv()
-            copies[c, 5, step].wait_recv()
+        wait(sq[c].at[0:7], recv.at[c, 3])
         left, right = xs[c][...].reshape(256, width), sq[c][...].reshape(128, width)
         product = (-6.0 / sample_total) * contract_cols(left[:, 0:count], right[:, 0:count])
         if c == GRAM:
@@ -205,35 +194,34 @@
                 dout[s][...] = total[s].reshape(4, 64, 128)
                 for step in (2, 1, 3):
                     there, device = along(g, step)
-                    copies["d", s, step] = start(
-                        dout[s].at[there], din[s].at[at[g]], d_send.at[s, step], d_recv.at[s, step], device
+                    start(
+                        dout[s].at[there], din[s].at[at[g]], d_send.at[s], d_recv.at[s], device
                     )
                 din[s][at[g]] = dout[s][at[g]]
-    for step in (1, 3, 2):
-        for s in range(2):
-            copies["d", s, step].wait_recv()
+    for s in range(2):
+        wait(din[s].at[0:3], d_recv.at[s])
     for chunk in range(4):
         rows_out[:, chunk] = (din[0][chunk] + din[1][chunk]).reshape(8, 8, 128)
-    done = []
     for order in range(7):
         there = jnp.where(samp < 4, 7 - order - jnp.where(7 - order <= samp, 1, 0), order + jnp.where(order >= samp, 1, 0))
         step = lax.rem(there + 8 - samp, 8)
         device = (feat, there)
-        done.append(start(
-            rows_out.at[there], rows_in.at[step - 1],
-            out_send.at[step - 1], out_recv.at[step - 1], device,
-        ))
-    for copy in started[:-7]:
-        copy.wait_send()
-    for copy in done:
-        copy.wait_recv()
+        start(rows_out.at[there], rows_in.at[step - 1], out_send, out_recv, device)
+    for s in range(2):
+        wait(fs[s].at[0:3], f_send.at[s])
+        wait(dout[s].at[0:3], d_send.at[s])
+    for c in range(n):
+        wait(xs[c].at[0:3], send.at[c, 0])
+        wait(got[c], send.at[c, 1])
+        wait(whole[c], send.at[c, 2])
+        wait(sq[c].at[0:7], send.at[c, 3])
+    wait(rows_in, out_recv)
     own = rows_out[samp]
     for slot in range(7):
         own = own + rows_in[slot]
     for chunk in range(4):
         o_ref[:, chunk * 128:(chunk + 1) * 128] = own[chunk]
-    for copy in done:
-        copy.wait_send()
+    wait(rows_in, out_send)
 
 
 def on_device(samples, factors):
@@ -246,18 +234,17 @@
     scratch = [pltpu.VMEM((64, 512), jnp.bfloat16)]
     scratch += each((4, 64), jnp.bfloat16)
     scratch += each((2, 4, 16), jnp.float32)
-    scratch += each((4, 16), jnp.float32)
-    scratch += each((3, 16), jnp.float32)
+    scratch += each((7, 16), jnp.float32)
     scratch += each((16,), jnp.float32)
     scratch += each((16,), jnp.float32)
-    scratch += each((2, 4, 16), jnp.bfloat16)
+    scratch += each((8, 16), jnp.bfloat16)
     scratch += [pltpu.VMEM((4, 64, 128), jnp.bfloat16)] * 2
     scratch += [pltpu.VMEM((4, 64, 128), jnp.float32)] * 4
     scratch += [pltpu.VMEM((8, 4, 8, 128), jnp.float32), pltpu.VMEM((7, 4, 8, 128), jnp.float32)]
     scratch += [pltpu.SemaphoreType.REGULAR((3,)), pltpu.SemaphoreType.DMA((n + 1,))]
-    scratch += [pltpu.SemaphoreType.DMA((2, 4))] * 4
-    scratch += [pltpu.SemaphoreType.DMA((n, 6, 4)), pltpu.SemaphoreType.DMA((n, 6, 4))]
-    scratch += [pltpu.SemaphoreType.DMA((7,)), pltpu.SemaphoreType.DMA((7,))]
+    scratch += [pltpu.SemaphoreType.DMA((2,))] * 4
+    scratch += [pltpu.SemaphoreType.DMA((n, 4))] * 2
+    scratch += [pltpu.SemaphoreType.DMA] * 2
     return pl.pallas_call(
         functools.partial(kernel, sample_total),
         out_shape=pltpu.VMEM((8, 512), jnp.float32),

time: 52 us -> 50.3 us (0.967); the launches traced: 51.7 us -> 49.4 us
  Pallas kernels: 51.1 us -> 48.8 us
    pallas_call x1, Pallas kernels: 51.1 us -> 48.8 us  [on_device(): pl.pallas_call(functools.partial(kernel, sample_total), out_shape=pltpu.V...]
where the time goes in v4:
time: 50.3 us; the launch traced here: 49.4 us
  Pallas kernels  48.8 us (97%)
  local copies, waits for them, and re-layouts  0.61 us (1%)
    pallas_call x1, Pallas kernels, on_device(): pl.pallas_call(functools.partial(kernel, sample_total), out_shape=pltpu.V...  48.8 us

profile of v4, /device:TPU:1, one launch (start us, length us, event | category | flops | bytes accessed | tf_op | source)
XLA Modules:
  0.0 49.4 jit_solution(2187176299054523532)
XLA Ops:
  0.0 48.8 %shard_map.28 = f32[8,512]{1,0:T(8,128)S(1)} custom-call(bf16[64,1024]{1,0:T(8,128)(2,1)} %x_ref.1, bf16[64,512]{1,0:T(8,128)(2,1)} %f_ref.1), custom_call_target="tpu_custom_call" | custom-call | flops 150994944 | bytes 1048576 | tf_op jit(solution)/shard_map/pallas_call | solution.py:248
  48.8 0.6 %copy.4 = f32[8,512]{1,0:T(8,128)} copy(f32[8,512]{1,0:T(8,128)S(1)} %shard_map.28) | data formatting | bytes 32768

commit v5 on v4

--- a/solution.py
+++ b/solution.py
@@ -65,6 +65,11 @@
     for load in loads:
         load.start()
     loads[0].wait()
+    column = lax.broadcasted_iota(jnp.int32, (512, 128), 1)
+    chosen = samp * 64 + jnp.where(column >= 64, column - 64, column)
+    pick = (lax.broadcasted_iota(jnp.int32, (512, 128), 0) == chosen).astype(jnp.bfloat16)
+    own_columns = jnp.dot(fv[...], pick, preferred_element_type=jnp.float32)
+    xs[GRAM][at[SIDES[0][0]], :, CHUNKS[GRAM][2]:] = own_columns.astype(jnp.bfloat16)
     for load in loads[1:]:
         load.wait()
     pl.semaphore_wait(barrier, len(partners))
@@ -94,12 +99,6 @@
                 fv.at[:, lanes], fs[s].at[at[g]], f_send.at[s], f_recv.at[s], device
             )
     for group in GROUPS:
-        if GRAM in group:
-            column = lax.broadcasted_iota(jnp.int32, (512, 128), 1)
-            chosen = samp * 64 + jnp.where(column >= 64, column - 64, column)
-            pick = (lax.broadcasted_iota(jnp.int32, (512, 128), 0) == chosen).astype(jnp.bfloat16)
-            own_columns = jnp.dot(fv[...], pick, preferred_element_type=jnp.float32)
-            xs[GRAM][at[SIDES[0][0]], :, CHUNKS[GRAM][2]:] = own_columns.astype(jnp.bfloat16)
         for step in (2, 1, 3):
             for c in group:
                 g = SIDES[CHUNKS[c][0]][0]

time: 50.3 us -> 49.8 us (0.990)
  no operation moved by 1% of the time
where the time goes in v5:
time: 49.8 us; the launch traced here: 49.4 us
  Pallas kernels  48.8 us (98%)
  local copies, waits for them, and re-layouts  0.61 us (1%)
    pallas_call x1, Pallas kernels, on_device(): pl.pallas_call(functools.partial(kernel, sample_total), out_shape=pltpu.V...  48.8 us

profile of v5, /device:TPU:1, one launch (start us, length us, event | category | flops | bytes accessed | tf_op | source)
XLA Modules:
  0.0 49.4 jit_solution(8894266849049424688)
XLA Ops:
  0.0 48.8 %shard_map.28 = f32[8,512]{1,0:T(8,128)S(1)} custom-call(bf16[64,1024]{1,0:T(8,128)(2,1)} %x_ref.1, bf16[64,512]{1,0:T(8,128)(2,1)} %f_ref.1), custom_call_target="tpu_custom_call" | custom-call | flops 150994944 | bytes 1048576 | tf_op jit(solution)/shard_map/pallas_call | solution.py:247
  48.8 0.6 %copy.4 = f32[8,512]{1,0:T(8,128)} copy(f32[8,512]{1,0:T(8,128)S(1)} %shard_map.28) | data formatting | bytes 32768

commit v6 on v5

--- a/solution.py
+++ b/solution.py
@@ -54,7 +54,7 @@
 
     barrier = pltpu.get_barrier_semaphore()
     partners = [along(axis, step, device)[1] for step in (2, 1, 3) for axis in "xy" for device in (feat, other_core)]
-    partners += [pair, beside(1), beside(-1)]
+    partners += [pair, beside(1), beside(-1), beside(2), beside(-2)]
     for device in partners:
         pl.semaphore_signal(barrier, inc=1, device_id=device, device_id_type=MESH)
     loads = [pltpu.make_async_copy(f_ref, fv, local_sem.at[n])]
@@ -76,12 +76,12 @@
 
     def tell(step):
         for device in (beside(step), beside(-step)):
-            pl.semaphore_signal(here.at[step // 2], inc=1, device_id=device, device_id_type=MESH)
+            pl.semaphore_signal(here.at[step // 4], inc=1, device_id=device, device_id_type=MESH)
 
     def hear(step):
-        pl.semaphore_wait(here.at[step // 2], 2)
-
-    tell(1)
+        pl.semaphore_wait(here.at[step // 4], 2)
+
+    tell(2)
     def start(src, dst, send_sem, recv_sem, device):
         pltpu.make_async_remote_copy(
             src_ref=src, dst_ref=dst, send_sem=send_sem, recv_sem=recv_sem,
@@ -109,8 +109,6 @@
 
     for s, (g, r) in enumerate(SIDES):
         fs[s][at[g]] = fv[:, pl.ds(pl.multiple_of(at[g] * 128, 128), 128)]
-    hear(1)
-    tell(2)
     weights = []
     for s in range(2):
         wait(fs[s].at[0:3], f_recv.at[s])
@@ -240,7 +238,7 @@
     scratch += [pltpu.VMEM((4, 64, 128), jnp.bfloat16)] * 2
     scratch += [pltpu.VMEM((4, 64, 128), jnp.float32)] * 4
     scratch += [pltpu.VMEM((8, 4, 8, 128), jnp.float32), pltpu.VMEM((7, 4, 8, 128), jnp.float32)]
-    scratch += [pltpu.SemaphoreType.REGULAR((3,)), pltpu.SemaphoreType.DMA((n + 1,))]
+    scratch += [pltpu.SemaphoreType.REGULAR((2,)), pltpu.SemaphoreType.DMA((n + 1,))]
     scratch += [pltpu.SemaphoreType.DMA((2,))] * 4
     scratch += [pltpu.SemaphoreType.DMA((n, 4))] * 2
     scratch += [pltpu.SemaphoreType.DMA] * 2

time: 49.8 us -> 50.1 us (level)
  no operation moved by 1% of the time
where the time goes in v6:
time: 50.1 us; the launch traced here: 49.9 us
  Pallas kernels  49.3 us (98%)
  local copies, waits for them, and re-layouts  0.61 us (1%)
    pallas_call x1, Pallas kernels, on_device(): pl.pallas_call(functools.partial(kernel, sample_total), out_shape=pltpu.V...  49.3 us

profile of v6, /device:TPU:1, one launch (start us, length us, event | category | flops | bytes accessed | tf_op | source)
XLA Modules:
  0.0 49.9 jit_solution(1234914107609455709)
XLA Ops:
  0.0 49.3 %shard_map.28 = f32[8,512]{1,0:T(8,128)S(1)} custom-call(bf16[64,1024]{1,0:T(8,128)(2,1)} %x_ref.1, bf16[64,512]{1,0:T(8,128)(2,1)} %f_ref.1), custom_call_target="tpu_custom_call" | custom-call | flops 150994944 | bytes 1048576 | tf_op jit(solution)/shard_map/pallas_call | solution.py:245
  49.3 0.6 %copy.4 = f32[8,512]{1,0:T(8,128)} copy(f32[8,512]{1,0:T(8,128)S(1)} %shard_map.28) | data formatting | bytes 32768
